TPU v7x, 32 devices: a whole 2x2x4 slice. The times are simulated.
32 devices in a mesh: req: 16 (over z, x, core), tp: 2 (over y).
Axes of the slice: x: 2, y: 2, z: 4, core: 2. Of those that a mesh axis runs over, the one named last changes fastest.
Arguments:
- queries: bfloat16 [2048, 8192], P('req', 'tp'), may hold values from -16 to 16
- span_rotated_keys: bfloat16 [2048, 1024], P('req', 'tp'), may hold values from -6 to 6
- span_token_values: bfloat16 [2048, 1024], P('req', 'tp'), may hold values from -6 to 6
- cache_keys: bfloat16 [16384, 1024], P('req', 'tp'), may hold values from -6 to 6
- prompt_cache_values: bfloat16 [16384, 1024], P('req', 'tp'), may hold values from -6 to 6
- lengths: int32 [2], replicated, may hold values from 2 to 8192, as said below
Outputs:
- attention: bfloat16 [2048, 8192], P(('req', 'tp'))
Inputs may be any that keep to these rules, and one draw needn't show every extreme that they name: `lengths`: each group's cached prompt length; one group's is exactly 8192.
All inputs are finite; a program needn't handle non-finite values.
Results may differ from a plain program's by a relative error of at most 0.0045.
Values may be sent and summed in bfloat16 or wider, within the bound.
A program may use at most 128 MiB of HBM per device.

v0:
```python
import math

import jax
import jax.numpy as jnp
from jax import lax
from jax.sharding import PartitionSpec as P

HEAD_SIZE = 128
GROUP_DEVS = 8


NEG_FILL = -1e30


def partner(value, axis, distance):
    mask = 2**distance
    pairs = [(source, source ^ mask) for source in range(lax.axis_size(axis))]
    return lax.ppermute(value, axis, pairs)


def heads_first(matrix, kv_heads):
    row_count = matrix.shape[0]
    return matrix.reshape(row_count, kv_heads, HEAD_SIZE).transpose(1, 0, 2)


def query_layout(query_block, kv_heads):
    token_count = query_block.shape[0]
    heads_per_group = query_block.shape[1] // (kv_heads * HEAD_SIZE)
    shaped = query_block.reshape(token_count, kv_heads, heads_per_group, HEAD_SIZE).transpose(
        1, 2, 0, 3
    )
    return shaped.reshape(kv_heads, heads_per_group * token_count, HEAD_SIZE)


def empty_state(kv_heads, row_count):
    return (
        jnp.full((kv_heads, row_count), NEG_FILL, jnp.float32),
        jnp.zeros((kv_heads, row_count), jnp.float32),
        jnp.zeros((kv_heads, row_count, HEAD_SIZE), jnp.float32),
    )


def absorb(online, query_rows, key_block, value_block, allowed):
    run_max, run_sum, run_acc = online
    scores = jnp.einsum(
        "jqd,jkd->jqk", query_rows, key_block, preferred_element_type=jnp.float32
    ) * (1.0 / math.sqrt(HEAD_SIZE))
    scores = jnp.where(allowed[None], scores, NEG_FILL)
    new_max = jnp.maximum(run_max, jnp.max(scores, axis=-1))
    weights = jnp.where(allowed[None], jnp.exp(scores - new_max[..., None]), 0.0)
    factor = jnp.exp(run_max - new_max)
    run_sum = run_sum * factor + jnp.sum(weights, axis=-1)
    run_acc = run_acc * factor[..., None] + jnp.einsum(
        "jqk,jkd->jqd",
        weights.astype(jnp.bfloat16),
        value_block,
        preferred_element_type=jnp.float32,
    )
    return (new_max, run_sum, run_acc)


def sweep(online, query_rows, key_rows, value_rows, live_rows, allowed_at):
    kv_heads = query_rows.shape[0]
    block_rows = math.gcd(key_rows.shape[0], 512)
    block_count = (live_rows + block_rows - 1) // block_rows

    def advance(block_index, inner_state):
        offset = block_index * block_rows
        key_block = heads_first(lax.dynamic_slice_in_dim(key_rows, offset, block_rows, 0), kv_heads)
        value_block = heads_first(
            lax.dynamic_slice_in_dim(value_rows, offset, block_rows, 0), kv_heads
        )
        return absorb(
            inner_state,
            query_rows,
            key_block,
            value_block,
            allowed_at(offset + jnp.arange(block_rows, dtype=jnp.int32)),
        )

    return lax.fori_loop(0, block_count, advance, online)


def cache_mask(first_row, group_length):

    def allowed_at(offsets):
        return (first_row + offsets < group_length)[None, :]

    return allowed_at


def span_mask(first_pos, query_pos):

    def allowed_at(offsets):
        return (first_pos + offsets)[None, :] <= query_pos[:, None]

    return allowed_at


def merge_parts(first_part, second_part):
    new_max = jnp.maximum(first_part[0], second_part[0])
    scale_one = jnp.exp(first_part[0] - new_max)
    scale_two = jnp.exp(second_part[0] - new_max)
    return (
        new_max,
        first_part[1] * scale_one + second_part[1] * scale_two,
        first_part[2] * scale_one[..., None] + second_part[2] * scale_two[..., None],
    )


def finish(online, token_count):
    run_max, run_sum, run_acc = online
    kv_heads = run_acc.shape[0]
    heads_per_group = run_acc.shape[1] // token_count
    output = run_acc / run_sum[..., None]
    output = output.reshape(kv_heads, heads_per_group, token_count, HEAD_SIZE).transpose(2, 0, 1, 3)
    return output.reshape(token_count, kv_heads * heads_per_group * HEAD_SIZE).astype(jnp.bfloat16)


def body(queries, span_rotated_keys, span_token_values, cache_keys, prompt_cache_values, lengths):
    kv_heads = span_rotated_keys.shape[1] // HEAD_SIZE
    tok_rows = queries.shape[0]
    cache_rows = cache_keys.shape[0]
    heads_per_group = queries.shape[1] // (kv_heads * HEAD_SIZE)
    bit_count = GROUP_DEVS.bit_length() - 1
    device = lax.axis_index("req")
    position = device % GROUP_DEVS
    group_length = lax.dynamic_index_in_dim(lengths, device // GROUP_DEVS, 0, keepdims=False)
    own_sets = queries
    for level in range(bit_count):
        peer_part = partner(own_sets, "req", level)
        mine_first = position >> level & 1 == 0
        own_sets = jnp.where(
            mine_first,
            jnp.concatenate([own_sets, peer_part], 0),
            jnp.concatenate([peer_part, own_sets], 0),
        )
    stacked = own_sets.reshape(GROUP_DEVS, tok_rows, own_sets.shape[1])
    first_row = position * cache_rows
    live_rows = jnp.clip(group_length - first_row, 0, cache_rows)

    def one_block(inputs):
        query_block, block_index = inputs
        query_rows = query_layout(query_block, kv_heads)
        query_pos = (
            block_index * tok_rows
            + jnp.arange(heads_per_group * tok_rows, dtype=jnp.int32) % tok_rows
        )
        online = empty_state(kv_heads, heads_per_group * tok_rows)
        online = sweep(
            online,
            query_rows,
            cache_keys,
            prompt_cache_values,
            live_rows,
            cache_mask(first_row, group_length),
        )
        return sweep(
            online,
            query_rows,
            span_rotated_keys,
            span_token_values,
            tok_rows,
            span_mask(position * tok_rows, query_pos),
        )

    partials = lax.map(one_block, (stacked, jnp.arange(GROUP_DEVS, dtype=jnp.int32)))
    for level in reversed(range(bit_count)):
        half_size = 1 << level
        upper_half = position >> level & 1 == 1
        kept_part = tuple(
            (jnp.where(upper_half, member[half_size:], member[:half_size]) for member in partials)
        )
        sent_part = tuple(
            (jnp.where(upper_half, member[:half_size], member[half_size:]) for member in partials)
        )
        gotten = partner(sent_part, "req", level)
        partials = merge_parts(kept_part, gotten)
    attended = finish(tuple((member[0] for member in partials)), tok_rows)
    return lax.all_to_all(attended, "tp", split_axis=0, concat_axis=1, tiled=True)


def solution(mesh):
    in_specs = (P("req", "tp"), P("req", "tp"), P("req", "tp"), P("req", "tp"), P("req", "tp"), P())
    out_specs = P(("req", "tp"), None)
    return jax.shard_map(body, mesh=mesh, in_specs=in_specs, out_specs=out_specs, check_vma=False)
```

profile of v0, /device:TPU:16, one launch (start us, length us, event | category | flops | bytes accessed | tf_op | source)
XLA Modules:
  0.0 862.8 jit_solution(1808783633657462442)
XLA Ops:
  6.7 46.3 %collective-permute-done.1 = bf16[256,4096]{1,0:T(8,128)(2,1)} collective-permute-done((bf16[256,4096]{1,0:T(8,128)(2,1)S(1)}, bf16[256,4096]{1,0:T(8,128)(2,1)}, u32[]{:S(2)}, u32[]{:S(2)}) %collective-permute-start.1) | collective-permute-done | bytes 2097184 | tf_op jit(solution)/shard_map/ppermute | solution.py:18
  64.3 85.5 %collective-permute-done.2 = bf16[512,4096]{1,0:T(8,128)(2,1)} collective-permute-done((bf16[512,4096]{1,0:T(8,128)(2,1)}, bf16[512,4096]{1,0:T(8,128)(2,1)}, u32[]{:S(2)}, u32[]{:S(2)}) %collective-permute-start.2) | collective-permute-done | bytes 4194336 | tf_op jit(solution)/shard_map/ppermute | solution.py:18
  149.8 11.1 %maximum_select_fusion = bf16[1024,4096]{1,0:T(8,128)(2,1)} fusion(bf16[512,4096]{1,0:T(8,128)(2,1)} %collective-permute-done.2, bf16[512,4096]{1,0:T(8,128)(2,1)} %maximum_select_fusion.1, pred[]{:T(512)S(6)} %eq.27), kind=kLoop, calls=%fused_computation.53 | loop fusion | flops 37748736 | bytes 16777216 | tf_op jit(solution)/shard_map/jit(_where)/select_n | solution.py:133
  160.9 364.9 %while.47 = (s32[]{:T(128)}, f32[8,4,1024]{2,1,0:T(4,128)S(1)}, f32[8,4,1024]{2,1,0:T(4,128)S(1)}, f32[8,4,1024,128]{3,2,1,0:T(8,128)}, bf16[8,128,4096]{2,1,0:T...) while((s32[]{:T(128)}, f32[8,4,1024]{2,1,0:T(4,128)S(1)}, ...), condition=%wide.region_7.8_spmd, body=%wide.region_0.7_spmd.sunk | while | flops 1378509440 | bytes 90468432 | solution.py:167
  168.5 31.1 %while.48 = (s32[]{:T(128)}, f32[4,1024]{1,0:T(4,128)S(1)}, f32[4,1024]{1,0:T(4,128)S(1)}, f32[4,1024,128]{2,1,0:T(8,128)}, s32[]{:T(128)}, /*index=5*/s32[]{:T(...) while((s32[]{:T(128)}, f32[4,1024]{1,0:T(4,128)S(1)}, ...), condition=%wide.region_4.4_spmd, body=%wide.region_1.3_spmd.sunk | while | flops 1102063104 | bytes 69470432 | solution.py:81
  175.7 8.4 multiply_add_fusion.10
  191.2 8.4 multiply_add_fusion.10
  214.1 31.1 %while.48 = (s32[]{:T(128)}, f32[4,1024]{1,0:T(4,128)S(1)}, f32[4,1024]{1,0:T(4,128)S(1)}, f32[4,1024,128]{2,1,0:T(8,128)}, s32[]{:T(128)}, /*index=5*/s32[]{:T(...) while((s32[]{:T(128)}, f32[4,1024]{1,0:T(4,128)S(1)}, ...), condition=%wide.region_4.4_spmd, body=%wide.region_1.3_spmd.sunk | while | flops 1102063104 | bytes 69470432 | solution.py:81
  221.2 8.4 multiply_add_fusion.10
  236.8 8.4 multiply_add_fusion.10
  259.7 31.1 %while.48 = (s32[]{:T(128)}, f32[4,1024]{1,0:T(4,128)S(1)}, f32[4,1024]{1,0:T(4,128)S(1)}, f32[4,1024,128]{2,1,0:T(8,128)}, s32[]{:T(128)}, /*index=5*/s32[]{:T(...) while((s32[]{:T(128)}, f32[4,1024]{1,0:T(4,128)S(1)}, ...), condition=%wide.region_4.4_spmd, body=%wide.region_1.3_spmd.sunk | while | flops 1102063104 | bytes 69470432 | solution.py:81
  266.8 8.4 multiply_add_fusion.10
  282.3 8.4 multiply_add_fusion.10
  305.3 31.1 %while.48 = (s32[]{:T(128)}, f32[4,1024]{1,0:T(4,128)S(1)}, f32[4,1024]{1,0:T(4,128)S(1)}, f32[4,1024,128]{2,1,0:T(8,128)}, s32[]{:T(128)}, /*index=5*/s32[]{:T(...) while((s32[]{:T(128)}, f32[4,1024]{1,0:T(4,128)S(1)}, ...), condition=%wide.region_4.4_spmd, body=%wide.region_1.3_spmd.sunk | while | flops 1102063104 | bytes 69470432 | solution.py:81
  327.9 8.4 multiply_add_fusion.10
  350.9 31.1 %while.48 = (s32[]{:T(128)}, f32[4,1024]{1,0:T(4,128)S(1)}, f32[4,1024]{1,0:T(4,128)S(1)}, f32[4,1024,128]{2,1,0:T(8,128)}, s32[]{:T(128)}, /*index=5*/s32[]{:T(...) while((s32[]{:T(128)}, f32[4,1024]{1,0:T(4,128)S(1)}, ...), condition=%wide.region_4.4_spmd, body=%wide.region_1.3_spmd.sunk | while | flops 1102063104 | bytes 69470432 | solution.py:81
  358.0 8.4 multiply_add_fusion.10
  373.5 8.4 multiply_add_fusion.10
  396.5 31.1 %while.48 = (s32[]{:T(128)}, f32[4,1024]{1,0:T(4,128)S(1)}, f32[4,1024]{1,0:T(4,128)S(1)}, f32[4,1024,128]{2,1,0:T(8,128)}, s32[]{:T(128)}, /*index=5*/s32[]{:T(...) while((s32[]{:T(128)}, f32[4,1024]{1,0:T(4,128)S(1)}, ...), condition=%wide.region_4.4_spmd, body=%wide.region_1.3_spmd.sunk | while | flops 1102063104 | bytes 69470432 | solution.py:81
  403.6 8.4 multiply_add_fusion.10
  419.2 8.4 multiply_add_fusion.10
  442.1 31.1 %while.48 = (s32[]{:T(128)}, f32[4,1024]{1,0:T(4,128)S(1)}, f32[4,1024]{1,0:T(4,128)S(1)}, f32[4,1024,128]{2,1,0:T(8,128)}, s32[]{:T(128)}, /*index=5*/s32[]{:T(...) while((s32[]{:T(128)}, f32[4,1024]{1,0:T(4,128)S(1)}, ...), condition=%wide.region_4.4_spmd, body=%wide.region_1.3_spmd.sunk | while | flops 1102063104 | bytes 69470432 | solution.py:81
  449.2 8.4 multiply_add_fusion.10
  464.7 8.4 multiply_add_fusion.10
  487.7 31.1 %while.48 = (s32[]{:T(128)}, f32[4,1024]{1,0:T(4,128)S(1)}, f32[4,1024]{1,0:T(4,128)S(1)}, f32[4,1024,128]{2,1,0:T(8,128)}, s32[]{:T(128)}, /*index=5*/s32[]{:T(...) while((s32[]{:T(128)}, f32[4,1024]{1,0:T(4,128)S(1)}, ...), condition=%wide.region_4.4_spmd, body=%wide.region_1.3_spmd.sunk | while | flops 1102063104 | bytes 69470432 | solution.py:81
  494.8 8.4 multiply_add_fusion.10
  510.3 8.4 multiply_add_fusion.10
  525.7 10.0 %slice_select_fusion = f32[4,4,1024,128]{3,2,1,0:T(8,128)} fusion(f32[8,4,1024,128]{3,2,1,0:T(8,128)} %get-tuple-element.385, pred[]{:T(512)S(6)} %eq.26), kind=kLoop, calls=%fused_computation.55 | loop fusion | flops 2097152 | bytes 25165824 | tf_op jit(solution)/shard_map/jit(_where)/select_n | solution.py:175
  539.6 179.3 %collective-permute-done.3 = f32[4,4,1024]{2,1,0:T(4,128)S(1)} collective-permute-done((f32[4,4,1024]{2,1,0:T(4,128)S(1)}, f32[4,4,1024]{2,1,0:T(4,128)S(1)}, u32[]{:S(2)}, u32[]{:S(2)}) %collective-permute-start.3) | collective-permute-done | bytes 65568 | tf_op jit(solution)/shard_map/ppermute | solution.py:18
  719.6 9.4 %multiply_add_fusion.2 = f32[4,4,1024,128]{3,2,1,0:T(8,128)S(1)} fusion(f32[4,4,1024,128]{3,2,1,0:T(8,128)} %collective-permute-done.4, f32[8,4,1024,128]{3,2,1,0:T(8,128)} %get-tuple-element.385, f32[4,4,1024]{2,1,0:T(4,128)S(1)} %get-tuple-element.508, f32[4,4,1024]{2,1,0:T(4,128)S(1)} %get-tuple-element.507, pred[]{:T(512)S(6)} %eq.26), kind=kLoop, calls=%fused_computation.54 | loop fusion | flops 8388608 | bytes 33685504 | tf_op jit(solution)/shard_map/add | solution.py:107
  737.2 87.7 %collective-permute-done.5 = f32[2,4,1024]{2,1,0:T(4,128)S(1)} collective-permute-done((f32[2,4,1024]{2,1,0:T(4,128)S(1)}, f32[2,4,1024]{2,1,0:T(4,128)S(1)}, u32[]{:S(2)}, u32[]{:S(2)}) %collective-permute-start.5) | collective-permute-done | bytes 32800 | tf_op jit(solution)/shard_map/ppermute | solution.py:18
  845.2 16.6 %all_to_all.16 = bf16[2,64,4096]{2,1,0:T(8,128)(2,1)S(1)} all-to-all(bf16[2,64,4096]{2,1,0:T(8,128)(2,1)S(1)} %convert_element_type.23), channel_id=1, replica_groups=mesh['req'=16,'tp'=2] {'tp'}, dimensions={0} | all-to-all | bytes 2097152 | tf_op jit(solution)/shard_map/all_to_all | solution.py:180
  (357 shorter events, 283.4 us)
Async XLA Ops:
  0.0 2.9 collective-permute-start
  5.1 47.8 %collective-permute-start.1 = (bf16[256,4096]{1,0:T(8,128)(2,1)S(1)}, bf16[256,4096]{1,0:T(8,128)(2,1)}, u32[]{:S(2)}, u32[]{:S(2)}) collective-permute-start(bf16[256,4096]{1,0:T(8,128)(2,1)S(1)} %maximum_select_fusion.2), channel_id=1, source_target_pairs={{0,4},{2,6},{4,0},{6,2},{8,12},{10,14},{12,8},{14,10},{16,20},{18,... | collective-permute-start | bytes 6291464 | tf_op jit(solution)/shard_map/ppermute | solution.py:18
  6.7 52.5 %copy-start.6 = (s32[2]{0:T(128)S(1)}, s32[2]{0:T(128)}, u32[]{:S(2)}) copy-start(s32[2]{0:T(128)} %param.15) | copy-start | bytes 28
  6.7 54.0 %copy-start.5 = (bf16[1024,512]{1,0:T(8,128)(2,1)S(1)}, bf16[1024,512]{1,0:T(8,128)(2,1)}, u32[]{:S(2)}) copy-start(bf16[1024,512]{1,0:T(8,128)(2,1)} %param.13) | copy-start | bytes 3145732
  57.7 92.1 %collective-permute-start.2 = (bf16[512,4096]{1,0:T(8,128)(2,1)}, bf16[512,4096]{1,0:T(8,128)(2,1)}, u32[]{:S(2)}, u32[]{:S(2)}) collective-permute-start(bf16[512,4096]{1,0:T(8,128)(2,1)} %maximum_select_fusion.1), channel_id=1, source_target_pairs={{0,8},{2,10},{4,12},{6,14},{8,0},{10,2},{12,4},{14,6},{16,24},{18,... | collective-permute-start | bytes 12582920 | tf_op jit(solution)/shard_map/ppermute | solution.py:18
  64.3 96.6 %copy-start.3 = (bf16[128,512]{1,0:T(8,128)(2,1)S(1)}, bf16[128,512]{1,0:T(8,128)(2,1)}, u32[]{:S(2)}) copy-start(bf16[128,512]{1,0:T(8,128)(2,1)} %param.11) | copy-start | bytes 393220
  64.3 96.6 %copy-start.4 = (bf16[128,512]{1,0:T(8,128)(2,1)S(1)}, bf16[128,512]{1,0:T(8,128)(2,1)}, u32[]{:S(2)}) copy-start(bf16[128,512]{1,0:T(8,128)(2,1)} %param.12) | copy-start | bytes 393220
  172.1 3.2 copy-start
  187.6 3.2 copy-start
  217.7 3.2 copy-start
  233.2 3.2 copy-start
  263.2 3.2 copy-start
  278.8 3.2 copy-start
  308.9 3.2 copy-start
  324.4 3.2 copy-start
  354.5 3.2 copy-start
  370.0 3.2 copy-start
  400.1 3.2 copy-start
  415.6 3.2 copy-start
  445.7 3.2 copy-start
  461.2 3.2 copy-start
  491.3 3.2 copy-start
  535.8 183.9 %collective-permute-start.4 = (f32[4,4,1024,128]{3,2,1,0:T(8,128)}, f32[4,4,1024,128]{3,2,1,0:T(8,128)}, u32[]{:S(2)}, u32[]{:S(2)}) collective-permute-start(f32[4,4,1024,128]{3,2,1,0:T(8,128)} %slice_select_fusion), channel_id=1, source_target_pairs={{0,8},{2,10},{4,12},{6,14},{8,0},{10,2},{12,4},{14,6},{16,24},{18,... | collective-permute-start | bytes 25165832 | tf_op jit(solution)/shard_map/ppermute | solution.py:18
  537.4 181.5 %collective-permute-start.3 = (f32[4,4,1024]{2,1,0:T(4,128)S(1)}, f32[4,4,1024]{2,1,0:T(4,128)S(1)}, u32[]{:S(2)}, u32[]{:S(2)}) collective-permute-start(f32[4,4,1024]{2,1,0:T(4,128)S(1)} %slice_select_fusion.4), channel_id=1, source_target_pairs={{0,8},{2,10},{4,12},{6,14},{8,0},{10,2},{12,4},{14,6},{16,24},{18,... | collective-permute-start | bytes 196616 | tf_op jit(solution)/shard_map/ppermute | solution.py:18
  537.9 181.6 %collective-permute-start.9 = (f32[4,4,1024]{2,1,0:T(4,128)S(1)}, f32[4,4,1024]{2,1,0:T(4,128)S(1)}, u32[]{:S(2)}, u32[]{:S(2)}) collective-permute-start(f32[4,4,1024]{2,1,0:T(4,128)S(1)} %slice_select_fusion.3), channel_id=1, source_target_pairs={{0,8},{2,10},{4,12},{6,14},{8,0},{10,2},{12,4},{14,6},{16,24},{18,... | collective-permute-start | bytes 196616 | tf_op jit(solution)/shard_map/ppermute | solution.py:18
  729.0 4.5 copy-start.1
  733.5 91.7 %collective-permute-start.6 = (f32[2,4,1024,128]{3,2,1,0:T(8,128)}, f32[2,4,1024,128]{3,2,1,0:T(8,128)}, u32[]{:S(2)}, u32[]{:S(2)}) collective-permute-start(f32[2,4,1024,128]{3,2,1,0:T(8,128)} %slice_select_fusion.1), channel_id=1, source_target_pairs={{0,4},{2,6},{4,0},{6,2},{8,12},{10,14},{12,8},{14,10},{16,20},{18,... | collective-permute-start | bytes 12582920 | tf_op jit(solution)/shard_map/ppermute | solution.py:18
  735.0 89.8 %collective-permute-start.5 = (f32[2,4,1024]{2,1,0:T(4,128)S(1)}, f32[2,4,1024]{2,1,0:T(4,128)S(1)}, u32[]{:S(2)}, u32[]{:S(2)}) collective-permute-start(f32[2,4,1024]{2,1,0:T(4,128)S(1)} %slice_select_fusion.7), channel_id=1, source_target_pairs={{0,4},{2,6},{4,0},{6,2},{8,12},{10,14},{12,8},{14,10},{16,20},{18,... | collective-permute-start | bytes 98312 | tf_op jit(solution)/shard_map/ppermute | solution.py:18
  735.6 89.6 %collective-permute-start.10 = (f32[2,4,1024]{2,1,0:T(4,128)S(1)}, f32[2,4,1024]{2,1,0:T(4,128)S(1)}, u32[]{:S(2)}, u32[]{:S(2)}) collective-permute-start(f32[2,4,1024]{2,1,0:T(4,128)S(1)} %slice_select_fusion.6), channel_id=1, source_target_pairs={{0,4},{2,6},{4,0},{6,2},{8,12},{10,14},{12,8},{14,10},{16,20},{18,... | collective-permute-start | bytes 98312 | tf_op jit(solution)/shard_map/ppermute | solution.py:18
  833.6 4.4 collective-permute-start.8
  833.7 3.8 collective-permute-start.7
  834.2 3.3 collective-permute-start.11
  (2 other events, 5.2 us)
where the time goes:
time: 864 us; the launch traced here: 863 us
  waiting for transfers between devices  406 us (47%)
  matrix products  209 us (24%)
  other arithmetic  124 us (14%)
  local copies, waits for them, and re-layouts  88.3 us (10%)
  blocking collectives  16.6 us (2%)
  starting transfers between devices  11.2 us (1%)
    ppermute x12, waiting for transfers between devices, partner(): return lax.ppermute(value, axis, pairs)  406 us
    dot_general x24, matrix products, absorb(): jnp.einsum('jqk,jkd->jqd', weights.astype(jnp.bfloat16), value_block, pre...  173 us
    reduce_sum x24, other arithmetic, absorb(): run_sum = run_sum * factor + jnp.sum(weights, axis=-1)  57.4 us
    dot_general x24, matrix products, absorb(): jnp.einsum('jqd,jkd->jqk', query_rows, key_block, preferred_element_type=...  36 us
    dynamic_slice x24, local copies, waits for them, and re-layouts, body(): lax.map(one_block, (stacked, jnp.arange(GROUP_DEVS, dtype=jnp.int32)))  20.8 us
    dynamic_slice x16, local copies, waits for them, and re-layouts, advance(): lax.dynamic_slice_in_dim(value_rows, offset, block_rows, 0)  20.3 us
    add x3, other arithmetic, merge_parts(): first_part[2] * scale_one[..., None] + second_part[2] * scale_two[..., None]  19.5 us
    select_n x3, other arithmetic, body(): jnp.where(mine_first, jnp.concatenate([own_sets, peer_part], 0), jnp.conc...  18 us
  transfers between devices with their start and end apart: 12, of which 9 were waited for; matrix products, arithmetic and copies ran while one was open for 1% of the time, Pallas kernels for 0%

commit v1 on v0

v1 whole, which is shorter than its diff:
```python
import functools
import math

import jax
import jax.numpy as jnp
from jax import lax
from jax.experimental import pallas as pl
from jax.experimental.pallas import tpu as pltpu
from jax.sharding import PartitionSpec as P

D = 128
KEY_BLOCK = 512
NEG_FILL = -1e30
LOG2_SCALE = math.log2(math.e) / math.sqrt(D)
MESH = pl.DeviceIdType.MESH


def kernel(
    n_tp,
    kv_heads,
    len_ref,
    q_ref,
    sk_ref,
    sv_ref,
    ck_ref,
    cv_ref,
    out_ref,
    q_buf,
    k_buf,
    kt_buf,
    v_buf,
    bias_buf,
    acc_buf,
    max_buf,
    part_out,
    part_in,
    lse_out,
    lse_in,
    merged,
    local_sem,
    kv_send,
    kv_recv,
    q_send,
    q_recv,
    part_send,
    part_recv,
    out_send,
    out_recv,
):
    tok = q_ref.shape[0]
    rows = ck_ref.shape[0]
    core_heads = q_buf.shape[2] // D
    width = core_heads * D
    kvh = k_buf.shape[0] // 2
    per_kv = core_heads // kvh
    part_width = per_kv * D
    pair_tok = 2 * tok
    cache = 2 * rows
    out_rows = out_ref.shape[0]

    r = lax.axis_index("req")
    t = lax.axis_index("tp")
    c = lax.rem(r, 2)
    x = lax.rem(lax.div(r, 2), 2)
    z = lax.rem(lax.div(r, 4), 2)
    g = lax.div(r, 8)

    def device(dz, dx, dc, dy=0):
        zz = 1 - z if dz else z
        xx = 1 - x if dx else x
        cc = 1 - c if dc else c
        return (g * 8 + zz * 4 + xx * 2 + cc, lax.rem(t + dy, n_tp) if dy else t)

    group_partners = [(0, 0, 1, 0), (0, 1, 0, 0), (0, 1, 1, 0), (1, 0, 0, 0), (1, 0, 1, 0)]
    out_partners = [(0, 0, 1, 0)]
    for dy in range(1, n_tp):
        out_partners += [(0, 0, 0, dy), (0, 0, 1, dy)]
    barrier = pltpu.get_barrier_semaphore()
    partners = group_partners + out_partners[1:]
    for partner in partners:
        pl.semaphore_signal(barrier, inc=1, device_id=device(*partner), device_id_type=MESH)

    for s in range(2 * kvh):
        v_buf[s, :, D:] = jnp.ones((cache + pair_tok, D), jnp.bfloat16)
    group_length = len_ref[g]
    for s in range(2):
        zz = z if s == 0 else 1 - z
        first = (zz * 4 + x * 2) * rows
        position = first + lax.broadcasted_iota(jnp.int32, (1, cache), 1)
        bias_buf[s] = jnp.where(position < group_length, 0.0, NEG_FILL)
    pl.semaphore_wait(barrier, len(partners))

    def kv_pieces(src, j, dest_core):
        col = j * D
        if kv_heads > 1:
            col = pl.multiple_of(dest_core * (kvh * D) + j * D, D)
        slot = src * kvh + j
        cache_at = pl.ds(pl.multiple_of(c * rows, 16), rows)
        span_at = pl.ds(pl.multiple_of(cache + c * tok, 16), tok)
        return [
            (ck_ref.at[:, pl.ds(col, D)], k_buf.at[slot, cache_at, :]),
            (sk_ref.at[:, pl.ds(col, D)], k_buf.at[slot, span_at, :]),
            (cv_ref.at[:, pl.ds(col, D)], v_buf.at[slot, cache_at, pl.ds(0, D)]),
            (sv_ref.at[:, pl.ds(col, D)], v_buf.at[slot, span_at, pl.ds(0, D)]),
        ]

    def q_piece(group_set, j, dest_core):
        col = pl.multiple_of(dest_core * width + j * part_width, D)
        return (
            q_ref.at[:, pl.ds(col, part_width)],
            q_buf.at[
                group_set, pl.ds(pl.multiple_of(c * tok, 16), tok), pl.ds(j * part_width, part_width)
            ],
        )

    def remote(pair, send, recv, dest):
        copy = pltpu.make_async_remote_copy(
            src_ref=pair[0],
            dst_ref=pair[1],
            send_sem=send,
            recv_sem=recv,
            device_id=dest,
            device_id_type=MESH,
        )
        copy.start()
        return copy

    locals_ = {}
    kv_copies = {}
    q_copies = {}

    def start_local(j):
        pairs = kv_pieces(0, j, c) + [q_piece(0, j, c)]
        copies = []
        for i, (src, dst) in enumerate(pairs):
            copy = pltpu.make_async_copy(src, dst, local_sem.at[j * 5 + i])
            copy.start()
            copies.append(copy)
        locals_[j] = copies

    def start_kv(way, j):
        dz, dc = ((0, 1), (1, 0), (1, 1))[way]
        pairs = kv_pieces(dz, j, 1 - c if dc else c)
        kv_copies[way, j] = [
            remote(
                pair,
                kv_send.at[(way * kvh + j) * 4 + i],
                kv_recv.at[(way * kvh + j) * 4 + i],
                device(dz, 0, dc),
            )
            for i, pair in enumerate(pairs)
        ]

    def start_q(way, j):
        dx, dc = ((0, 1), (1, 0), (1, 1))[way]
        q_copies[way, j] = remote(
            q_piece(dx, j, 1 - c if dc else c),
            q_send.at[way * kvh + j],
            q_recv.at[way * kvh + j],
            device(0, dx, dc),
        )

    for j in range(kvh):
        start_local(j)
        start_q(0, j)
        start_kv(0, j)
        start_q(1, j)
        start_q(2, j)
        start_kv(1, j)
        start_kv(2, j)

    def unit(group_set, src, j):
        slot = src * kvh + j
        q_first = (z * 4 + (x if group_set == 0 else 1 - x) * 2) * tok
        k_first = ((z if src == 0 else 1 - z) * 4 + x * 2) * tok
        ahead = (
            q_first
            - k_first
            + lax.broadcasted_iota(jnp.int32, (pair_tok, pair_tok), 0)
            - lax.broadcasted_iota(jnp.int32, (pair_tok, pair_tok), 1)
        )

        def one_head(h, carry):
            head = group_set * core_heads + j * per_kv + h
            q = q_buf[
                group_set, :, pl.ds(pl.multiple_of(j * part_width + h * D, D), D)
            ]
            run_max = acc = None
            if src == 1:
                run_max = max_buf[head][:, :1]
                acc = acc_buf[head]
            block = math.gcd(KEY_BLOCK, cache)
            spans = [(b * block, block) for b in range(cache // block)] + [(cache, pair_tok)]
            for start, size in spans:
                scores = (
                    jnp.dot(
                        q,
                        kt_buf[slot, :, start : start + size],
                        preferred_element_type=jnp.float32,
                    )
                    * LOG2_SCALE
                )
                if start < cache:
                    scores = scores + bias_buf[src, :, start : start + size]
                else:
                    scores = jnp.where(ahead >= 0, scores, NEG_FILL)
                top = jnp.max(scores, axis=1, keepdims=True)
                new_max = top if run_max is None else jnp.maximum(run_max, top)
                weights = jnp.exp2(scores - new_max).astype(jnp.bfloat16)
                term = jnp.dot(
                    weights,
                    v_buf[slot, start : start + size, :],
                    preferred_element_type=jnp.float32,
                )
                acc = term if run_max is None else acc * jnp.exp2(run_max - new_max) + term
                run_max = new_max
            if src == 1 and group_set == 1:
                total = acc[:, D : D + 1]
                part_out[j, :, pl.ds(pl.multiple_of(h * D, D), D)] = (acc[:, :D] / total).astype(
                    jnp.bfloat16
                )
                lane = lax.broadcasted_iota(jnp.int32, (pair_tok, D), 1)
                lse_out[j] = jnp.where(lane == h, run_max + jnp.log2(total), lse_out[j])
            else:
                acc_buf[head] = acc
                max_buf[head] = jnp.broadcast_to(run_max, (pair_tok, D))
            return carry

        lax.fori_loop(0, per_kv, one_head, 0)

    def turn_keys(src, j):
        slot = src * kvh + j
        kt_buf[slot] = k_buf[slot].T

    for j in range(kvh):
        lse_out[j] = jnp.zeros((pair_tok, D), jnp.float32)

    for j in range(kvh):
        for copy in locals_[j]:
            copy.wait()
        for copy in kv_copies[0, j] + [q_copies[0, j]]:
            copy.wait_recv()
        turn_keys(0, j)
        unit(0, 0, j)
    for j in range(kvh):
        q_copies[1, j].wait_recv()
        q_copies[2, j].wait_recv()
        unit(1, 0, j)
    part_copies = []
    for j in range(kvh):
        for copy in kv_copies[1, j] + kv_copies[2, j]:
            copy.wait_recv()
        turn_keys(1, j)
        unit(1, 1, j)
        for i, (src, dst) in enumerate(((part_out, part_in), (lse_out, lse_in))):
            part_copies.append(
                remote(
                    (src.at[j], dst.at[j]),
                    part_send.at[2 * j + i],
                    part_recv.at[2 * j + i],
                    device(0, 1, 0),
                )
            )
        unit(0, 1, j)
    out_copies = []
    out_locals = []
    for j in range(kvh):
        part_copies[2 * j].wait_recv()
        part_copies[2 * j + 1].wait_recv()

        def merge(h, carry):
            head = j * per_kv + h
            lane = lax.broadcasted_iota(jnp.int32, (pair_tok, D), 1)
            other = jnp.sum(jnp.where(lane == h, lse_in[j], 0.0), axis=1, keepdims=True)
            own_max = max_buf[head][:, :1]
            top = jnp.maximum(own_max, other)
            own = jnp.exp2(own_max - top)
            theirs = jnp.exp2(other - top)
            cols = pl.ds(pl.multiple_of(h * D, D), D)
            acc = acc_buf[head]
            total = acc[:, D : D + 1] * own + theirs
            value = acc[:, :D] * own + part_in[j, :, cols].astype(jnp.float32) * theirs
            merged[j, :, cols] = (value / total).astype(jnp.bfloat16)
            return carry

        lax.fori_loop(0, per_kv, merge, 0)
        col = pl.multiple_of(t * (2 * width) + c * width + j * part_width, D)
        for i, partner in enumerate([(0, 0, 0, 0)] + out_partners):
            dest = device(*partner)
            dest_core = 1 - c if partner[2] else c
            src = merged.at[
                j, pl.ds(pl.multiple_of(dest_core * tok + dest[1] * out_rows, 16), out_rows), :
            ]
            dst = out_ref.at[:, pl.ds(col, part_width)]
            if i == 0:
                copy = pltpu.make_async_copy(src, dst, local_sem.at[5 * kvh + j])
                copy.start()
                out_locals.append(copy)
            else:
                k = j * len(out_partners) + i - 1
                out_copies.append(remote((src, dst), out_send.at[k], out_recv.at[k], dest))

    for copy in out_locals:
        copy.wait()
    for copy in out_copies:
        copy.wait_recv()
    for copies in kv_copies.values():
        for copy in copies:
            copy.wait_send()
    for copy in list(q_copies.values()) + part_copies + out_copies:
        copy.wait_send()


def body(n_tp, queries, span_keys, span_values, cache_keys, cache_values, lengths):
    tok = queries.shape[0]
    rows = cache_keys.shape[0]
    kv_heads = cache_keys.shape[1] // D
    kvh = max(1, kv_heads // 2)
    core_heads = queries.shape[1] // D // 2
    part_width = core_heads // kvh * D
    pair_tok, keys = 2 * tok, 2 * (rows + tok)
    n_out = 1 + 2 * (n_tp - 1)
    dma = pltpu.SemaphoreType.DMA
    any_spec = pl.BlockSpec(memory_space=pl.ANY)
    return pl.pallas_call(
        functools.partial(kernel, n_tp, kv_heads),
        out_shape=jax.ShapeDtypeStruct((tok // n_tp, queries.shape[1] * n_tp), jnp.bfloat16),
        in_specs=[pl.BlockSpec(memory_space=pltpu.SMEM)] + [any_spec] * 5,
        out_specs=any_spec,
        scratch_shapes=[
            pltpu.VMEM((2, pair_tok, core_heads * D), jnp.bfloat16),
            pltpu.VMEM((2 * kvh, keys, D), jnp.bfloat16),
            pltpu.VMEM((2 * kvh, D, keys), jnp.bfloat16),
            pltpu.VMEM((2 * kvh, keys, 2 * D), jnp.bfloat16),
            pltpu.VMEM((2, 1, 2 * rows), jnp.float32),
            pltpu.VMEM((2 * core_heads, pair_tok, 2 * D), jnp.float32),
            pltpu.VMEM((2 * core_heads, pair_tok, D), jnp.float32),
            pltpu.VMEM((kvh, pair_tok, part_width), jnp.bfloat16),
            pltpu.VMEM((kvh, pair_tok, part_width), jnp.bfloat16),
            pltpu.VMEM((kvh, pair_tok, D), jnp.float32),
            pltpu.VMEM((kvh, pair_tok, D), jnp.float32),
            pltpu.VMEM((kvh, pair_tok, part_width), jnp.bfloat16),
            dma((6 * kvh,)),
            dma((12 * kvh,)),
            dma((12 * kvh,)),
            dma((3 * kvh,)),
            dma((3 * kvh,)),
            dma((2 * kvh,)),
            dma((2 * kvh,)),
            dma((n_out * kvh,)),
            dma((n_out * kvh,)),
        ],
        compiler_params=pltpu.CompilerParams(
            collective_id=0, has_side_effects=True, vmem_limit_bytes=52 << 20
        ),
        name="spanned_attention",
    )(lengths, queries, span_keys, span_values, cache_keys, cache_values)


def solution(mesh):
    in_specs = (P("req", "tp"), P("req", "tp"), P("req", "tp"), P("req", "tp"), P("req", "tp"), P())
    out_specs = P(("req", "tp"), None)
    return jax.shard_map(
        functools.partial(body, mesh.shape["tp"]),
        mesh=mesh,
        in_specs=in_specs,
        out_specs=out_specs,
        check_vma=False,
    )
```

time: 864 us -> 112 us (0.13)
  waiting for transfers between devices: 406 us -> 0 us
  matrix products: 209 us -> 0 us
  other arithmetic: 124 us -> 0 us
  Pallas kernels: 0 us -> 107 us
  local copies, waits for them, and re-layouts: 88.3 us -> 3.43 us
  blocking collectives: 16.6 us -> 0 us
  starting transfers between devices: 11.2 us -> 0 us
    ppermute x12 -> x0, waiting for transfers between devices: 406 us -> none  [partner(): return lax.ppermute(value, axis, pairs)]
    dot_general x48 -> x0, matrix products: 209 us -> none  [the longest x24 173 us: absorb(): jnp.einsum('jqk,jkd->jqd', weights.astype(jnp.bfloat16), value_block, pre...]
    pallas_call x0 -> x1, Pallas kernels: none -> 107 us  [body(): pl.pallas_call(functools.partial(kernel, n_tp, kv_heads), out_shape=jax.S...]
    reduce_sum x24 -> x0, other arithmetic: 57.4 us -> none  [absorb(): run_sum = run_sum * factor + jnp.sum(weights, axis=-1)]
    dynamic_slice x41 -> x0, local copies, waits for them, and re-layouts: 41.8 us -> none  [the longest x24 20.8 us: body(): lax.map(one_block, (stacked, jnp.arange(GROUP_DEVS, dtype=jnp.int32)))]
    select_n x12 -> x0, other arithmetic: 31 us -> none  [the longest x3 18 us: body(): jnp.where(mine_first, jnp.concatenate([own_sets, peer_part], 0), jnp.conc...]
    add x37 -> x0, other arithmetic: 20.1 us -> none  [the longest x3 19.5 us: merge_parts(): first_part[2] * scale_one[..., None] + second_part[2] * scale_two[..., None]]
    all_to_all x1 -> x0, blocking collectives: 16.6 us -> none  [body(): lax.all_to_all(attended, 'tp', split_axis=0, concat_axis=1, tiled=True)]
  transfers between devices with their start and end apart: 12 -> 0, of which waited for: 9 -> 0; matrix products, arithmetic and copies ran while one was open for 1% -> 0% of each run, Pallas kernels for 0% -> 0%
where the time goes in v1:
time: 112 us; the launch traced here: 110 us
  Pallas kernels  107 us (96%)
  local copies, waits for them, and re-layouts  3.43 us (3%)
    pallas_call x1, Pallas kernels, body(): pl.pallas_call(functools.partial(kernel, n_tp, kv_heads), out_shape=jax.S...  107 us
    unnamed x7, local copies, waits for them, and re-layouts  3.43 us

profile of v1, /device:TPU:16, one launch (start us, length us, event | category | flops | bytes accessed | tf_op | source)
XLA Modules:
  0.0 110.0 jit_solution(11794538984595455500)
XLA Ops:
  0.0 0.0 copy-start
  0.0 0.9 copy-done
  0.9 0.0 copy-start.1
  0.9 0.9 copy-done.1
  1.8 0.0 copy-start.2
  1.8 0.7 copy-done.2
  2.5 106.6 %spanned_attention.1 = bf16[64,8192]{1,0:T(8,128)(2,1)S(1)} custom-call(s32[2]{0:T(128)S(1)} %copy-done.2, bf16[128,4096]{1,0:T(8,128)(2,1)} %q_ref.1, bf16[128,512]{1,0:T(8,128)(2,1)S(1)} %copy-done, bf16[128,512]{1,0:T(8,128)(2,1)S(1)} %copy-done.1, bf16[1024,512]{1,0:T(8,128)(2,1)} %ck_ref.1, bf16[1024,512]{1,0:T(8,128)(2,1)} %cv_ref.1), custom_call_target="tpu_custom_call" | custom-call | tf_op jit(solution)/shard_map/spanned_attention/pallas_call | solution.py:325
  109.1 1.0 copy.8
Async XLA Ops:
  0.0 0.9 copy-start
  0.9 0.9 copy-start.1
  1.8 0.7 copy-start.2

commit v2 on v1

--- a/solution.py
+++ b/solution.py
@@ -226,7 +226,7 @@
                 max_buf[head] = jnp.broadcast_to(run_max, (pair_tok, D))
             return carry
 
-        lax.fori_loop(0, per_kv, one_head, 0)
+        lax.fori_loop(0, per_kv, one_head, 0, unroll=2)
 
     def turn_keys(src, j):
         slot = src * kvh + j

time: 112 us -> 108 us (0.964)
  Pallas kernels: 107 us -> 103 us
    pallas_call x1, Pallas kernels: 107 us -> 103 us  [body(): pl.pallas_call(functools.partial(kernel, n_tp, kv_heads), out_shape=jax.S...]
where the time goes in v2:
time: 108 us; the launch traced here: 107 us
  Pallas kernels  103 us (95%)
  local copies, waits for them, and re-layouts  3.43 us (3%)
    pallas_call x1, Pallas kernels, body(): pl.pallas_call(functools.partial(kernel, n_tp, kv_heads), out_shape=jax.S...  103 us
    unnamed x7, local copies, waits for them, and re-layouts  3.43 us

profile of v2, /device:TPU:16, one launch (start us, length us, event | category | flops | bytes accessed | tf_op | source)
XLA Modules:
  0.0 106.7 jit_solution(11410097040573266400)
XLA Ops:
  0.0 0.0 copy-start
  0.0 0.9 copy-done
  0.9 0.0 copy-start.1
  0.9 0.9 copy-done.1
  1.8 0.0 copy-start.2
  1.8 0.7 copy-done.2
  2.5 103.2 %spanned_attention.1 = bf16[64,8192]{1,0:T(8,128)(2,1)S(1)} custom-call(s32[2]{0:T(128)S(1)} %copy-done.2, bf16[128,4096]{1,0:T(8,128)(2,1)} %q_ref.1, bf16[128,512]{1,0:T(8,128)(2,1)S(1)} %copy-done, bf16[128,512]{1,0:T(8,128)(2,1)S(1)} %copy-done.1, bf16[1024,512]{1,0:T(8,128)(2,1)} %ck_ref.1, bf16[1024,512]{1,0:T(8,128)(2,1)} %cv_ref.1), custom_call_target="tpu_custom_call" | custom-call | tf_op jit(solution)/shard_map/spanned_attention/pallas_call | solution.py:325
  105.7 1.0 copy.8
Async XLA Ops:
  0.0 0.9 copy-start
  0.9 0.9 copy-start.1
  1.8 0.7 copy-start.2
